TPU v7x, 256 devices: a whole 4x4x8 slice. The times are simulated.
256 devices in a mesh: seq: 32 (over y, z), head: 8 (over x, core).
Axes of the slice: x: 4, y: 4, z: 8, core: 2. Of those that a mesh axis runs over, the one named last changes fastest.
Arguments:
- queries: bfloat16 [65536, 2048], P('seq', 'head'), may hold values from -2.5 to 2.5
- keys: bfloat16 [65536, 2048], P('seq', 'head'), may hold values from -2.5 to 2.5
- values: bfloat16 [65536, 2048], P('seq', 'head'), may hold values from -2.5 to 2.5
- w_out: bfloat16 [2048, 2048], P('head'), may hold values from -0.125 to 0.125
- grad_out: bfloat16 [65536, 2048], P(('seq', 'head')), may hold values from -6 to 6
Outputs:
- mixed: bfloat16 [65536, 2048], P(('seq', 'head'))
- grad_queries: bfloat16 [65536, 2048], P('seq', 'head')
- grad_keys: bfloat16 [65536, 2048], P('seq', 'head')
- grad_values: bfloat16 [65536, 2048], P('seq', 'head')
- grad_weight: bfloat16 [2048, 2048], P('head')
All inputs are finite; a program needn't handle non-finite values.
Results may differ from a plain program's by a relative error of at most 0.013.
Values may be sent and summed in bfloat16 or wider, within the bound.
No kernel may reach another device: no remote copies, remote signals or barrier semaphores. Data moves between devices by JAX's collectives and lax.ppermute only.
A program may use at most 192 MiB of HBM per device.

v0:
```python
import jax
import jax.numpy as jnp
from jax import lax
from jax.sharding import PartitionSpec as P

HEAD_DIM = 128
B = 128


def from_partner(block, axis, bit):
    count = lax.axis_size(axis)
    route = []
    for low in range(count):
        high = low | 1 << bit
        if high != low and high < count:
            route += [(low, high), (high, low)]
    return lax.ppermute(block, axis, route)


def pair_mean(stacked):
    dims_in = stacked.shape
    pairs = stacked.reshape(dims_in[:-2] + (dims_in[-2] // 2, 2, dims_in[-1])).astype(jnp.float32)
    return ((pairs[..., 0, :] + pairs[..., 1, :]) * 0.5).astype(jnp.bfloat16)


def pair_sum(matrix):
    dims_in = matrix.shape
    pairs = matrix.reshape((dims_in[0] // 2, 2) + dims_in[1:])
    return pairs[:, 0] + pairs[:, 1]


def swap_blocks(blocks):
    dims_in = blocks.shape
    return blocks.reshape((dims_in[0] // 2, 2) + dims_in[1:])[:, ::-1].reshape(dims_in)


def spread(matrix, repeats):
    dims_in = matrix.shape
    widened = jnp.broadcast_to(matrix[:, None], (dims_in[0], repeats) + dims_in[1:])
    return widened.reshape((dims_in[0] * repeats,) + dims_in[1:])


def as_blocks(matrix, block_rows, head_count):
    return matrix.reshape(
        matrix.shape[0] // block_rows, block_rows, head_count, matrix.shape[1] // head_count
    )


def as_rows(blocks):
    return blocks.reshape(blocks.shape[0] * blocks.shape[1], blocks.shape[2] * blocks.shape[3])


def forward_terms(query_blocks, key_blocks, value_blocks, weight, scale):
    scores = (
        jnp.einsum("nqhd,nkhd->nhqk", query_blocks, key_blocks, preferred_element_type=jnp.float32)
        * scale
    )
    expos = jnp.exp(scores)
    totals = jnp.transpose(weight * jnp.sum(expos, axis=-1), (0, 2, 1))
    numers = weight * jnp.einsum(
        "nhqk,nkhd->nqhd",
        expos.astype(jnp.bfloat16),
        value_blocks,
        preferred_element_type=jnp.float32,
    )
    return (
        as_rows(numers),
        totals.reshape(totals.shape[0] * totals.shape[1], totals.shape[2]),
        expos,
    )


def backward_terms(
    query_blocks, key_blocks, value_blocks, expos, grad_blocks, dot_blocks, weight, scale
):
    probe = jnp.einsum(
        "nqhd,nkhd->nhqk", grad_blocks, value_blocks, preferred_element_type=jnp.float32
    )
    slopes = (weight * expos * (probe - jnp.transpose(dot_blocks, (0, 2, 1))[..., None])).astype(
        jnp.bfloat16
    )
    grad_query = scale * jnp.einsum(
        "nhqk,nkhd->nqhd", slopes, key_blocks, preferred_element_type=jnp.float32
    )
    grad_key = scale * jnp.einsum(
        "nhqk,nqhd->nkhd", slopes, query_blocks, preferred_element_type=jnp.float32
    )
    grad_value = weight * jnp.einsum(
        "nhqk,nqhd->nkhd",
        expos.astype(jnp.bfloat16),
        grad_blocks,
        preferred_element_type=jnp.float32,
    )
    return (grad_query, grad_key, grad_value)


def body(queries, keys, values, w_out, grad_out):
    tokens_here = queries.shape[0]
    width = queries.shape[1]
    heads_here = width // HEAD_DIM
    scale = HEAD_DIM ** (-0.5)
    local_bits = (tokens_here // B).bit_length() - 1
    seq_bits = lax.axis_size("seq").bit_length() - 1
    position = lax.axis_index("seq")
    level_count = local_bits + seq_bits
    q_levels = [queries]
    k_levels = [keys]
    v_levels = [values]
    for level in range(1, level_count):
        q_levels.append(pair_mean(q_levels[-1]))
        k_levels.append(pair_mean(k_levels[-1]))
        v_levels.append(pair_mean(v_levels[-1]))
    numer = jnp.zeros((tokens_here, width), jnp.float32)
    total = jnp.zeros((tokens_here, heads_here), jnp.float32)
    local_saved = []
    for level in range(local_bits):
        weight = 2.0**level
        query_blocks = as_blocks(q_levels[level], B, heads_here)
        key_blocks = as_blocks(k_levels[level], B, heads_here)
        value_blocks = as_blocks(v_levels[level], B, heads_here)
        pairings = [(swap_blocks(key_blocks), swap_blocks(value_blocks), True)]
        if level == 0:
            pairings.append((key_blocks, value_blocks, False))
        for key_side, value_side, swapped in pairings:
            level_numer, level_total, expos = forward_terms(
                query_blocks, key_side, value_side, weight, scale
            )
            numer = numer + spread(level_numer, 2**level)
            total = total + spread(level_total, 2**level)
            local_saved.append((level, key_side, value_side, swapped, expos))
    remote_saved = []
    group = jnp.stack([k_levels[local_bits], v_levels[local_bits]])
    sibling = group
    for section in range(seq_bits):
        level = local_bits + section
        weight = 2.0**level
        group = jnp.stack([k_levels[level], v_levels[level]])
        for bit_pos in range(section):
            other = from_partner(group, "seq", bit_pos)
            upper_side = position // 2**bit_pos % 2 == 1
            group = jnp.where(
                upper_side,
                jnp.concatenate([other, group], axis=1),
                jnp.concatenate([group, other], axis=1),
            )
        sibling = from_partner(group, "seq", section)
        own_rows = q_levels[level].shape[0]
        query_blocks = as_blocks(q_levels[level], own_rows, heads_here)
        key_side = as_blocks(sibling[0], sibling.shape[1], heads_here)
        value_side = as_blocks(sibling[1], sibling.shape[1], heads_here)
        level_numer, level_total, expos = forward_terms(
            query_blocks, key_side, value_side, weight, scale
        )
        numer = numer + spread(level_numer, 2**level)
        total = total + spread(level_total, 2**level)
        remote_saved.append((section, query_blocks, key_side, value_side, expos))
    attended = (
        (numer.reshape(tokens_here, heads_here, HEAD_DIM) / total[:, :, None])
        .reshape(tokens_here, width)
        .astype(jnp.bfloat16)
    )
    rows_here = attended
    mixed = lax.psum_scatter(
        jnp.dot(rows_here, w_out, preferred_element_type=jnp.float32),
        "head",
        scatter_dimension=0,
        tiled=True,
    )
    mixed = mixed.astype(jnp.bfloat16)
    piece = lax.all_gather(grad_out, "head", axis=0, tiled=True)
    part_rows = lax.dot_general(
        piece, w_out, (((1,), (1,)), ((), ())), preferred_element_type=jnp.float32
    )
    rows_here = attended
    grad_proj = lax.dot_general(
        rows_here, piece, (((0,), (0,)), ((), ())), preferred_element_type=jnp.float32
    )
    grad_attended, grad_proj = (part_rows, grad_proj)
    grad_weight = lax.psum(grad_proj, "seq").astype(jnp.bfloat16)
    dot_rows = jnp.sum(
        (grad_attended * attended.astype(jnp.float32)).reshape(tokens_here, heads_here, HEAD_DIM),
        axis=-1,
    )
    g_levels = [
        (grad_attended.reshape(tokens_here, heads_here, HEAD_DIM) / total[:, :, None]).reshape(
            tokens_here, width
        )
    ]
    h_levels = [dot_rows / total]
    for level in range(1, level_count):
        g_levels.append(pair_sum(g_levels[-1]))
        h_levels.append(pair_sum(h_levels[-1]))
    grad_q = jnp.zeros((tokens_here, width), jnp.float32)
    grad_k = jnp.zeros((tokens_here, width), jnp.float32)
    grad_v = jnp.zeros((tokens_here, width), jnp.float32)
    for level, key_side, value_side, swapped, expos in local_saved:
        weight = 2.0**level
        query_blocks = as_blocks(q_levels[level], B, heads_here)
        grad_blocks = as_blocks(g_levels[level].astype(jnp.bfloat16), B, heads_here)
        dot_blocks = h_levels[level].reshape(-1, B, heads_here)
        level_q, level_k, level_v = backward_terms(
            query_blocks, key_side, value_side, expos, grad_blocks, dot_blocks, weight, scale
        )
        if swapped:
            level_k = swap_blocks(level_k)
            level_v = swap_blocks(level_v)
        grad_q = grad_q + spread(as_rows(level_q), 2**level) / weight
        grad_k = grad_k + spread(as_rows(level_k), 2**level) / weight
        grad_v = grad_v + spread(as_rows(level_v), 2**level) / weight
    for section, query_blocks, key_side, value_side, expos in remote_saved:
        level = local_bits + section
        weight = 2.0**level
        own_rows = q_levels[level].shape[0]
        grad_blocks = as_blocks(g_levels[level].astype(jnp.bfloat16), own_rows, heads_here)
        dot_blocks = h_levels[level].reshape(1, own_rows, heads_here)
        level_q, level_k, level_v = backward_terms(
            query_blocks, key_side, value_side, expos, grad_blocks, dot_blocks, weight, scale
        )
        grad_q = grad_q + spread(as_rows(level_q), 2**level) / weight
        returned = jnp.stack([as_rows(level_k), as_rows(level_v)])
        for bit_pos in range(section - 1, -1, -1):
            half_rows = returned.shape[1] // 2
            lower = returned[:, :half_rows]
            upper = returned[:, half_rows:]
            upper_side = position // 2**bit_pos % 2 == 1
            kept = jnp.where(upper_side, upper, lower)
            handed = jnp.where(upper_side, lower, upper)
            returned = kept + from_partner(handed, "seq", bit_pos)
        returned = from_partner(returned, "seq", section)
        grad_k = grad_k + spread(returned[0], 2**level) / weight
        grad_v = grad_v + spread(returned[1], 2**level) / weight
    return (
        mixed,
        grad_q.astype(jnp.bfloat16),
        grad_k.astype(jnp.bfloat16),
        grad_v.astype(jnp.bfloat16),
        grad_weight,
    )


def solution(mesh):
    return jax.shard_map(
        body,
        mesh=mesh,
        in_specs=(
            P("seq", "head"),
            P("seq", "head"),
            P("seq", "head"),
            P("head", None),
            P(("seq", "head"), None),
        ),
        out_specs=(
            P(("seq", "head"), None),
            P("seq", "head"),
            P("seq", "head"),
            P("seq", "head"),
            P("head", None),
        ),
        check_vma=False,
    )
```

profile of v0, /device:TPU:16, one launch (start us, length us, event | category | flops | bytes accessed | tf_op | source)
XLA Modules:
  0.0 820.7 jit_solution(3838982992629274795)
XLA Ops:
  22.5 4.0 fusion.227
  28.2 4.4 convert_reduce_fusion.1
  55.7 4.0 fusion.229
  71.9 3.6 convert_reduce_fusion.2
  86.4 3.4 convert_reduce_fusion.5
  106.6 3.3 convert_reduce_fusion.7
  153.4 3.2 reshape.1575
  156.7 4.6 copy.1289
  164.3 3.7 reshape.1572
  168.8 3.4 collective-permute-start.11
  173.9 6.9 collective-permute-start.12
  191.3 3.1 collective-permute-start.5
  255.1 5.6 div.296
  260.8 11.2 %convert_multiply_fusion = (f32[2048,256]{1,0:T(8,128)}, bf16[2048,256]{1,0:T(8,128)(2,1)S(1)}, bf16[2048,256]{1,0:T(8,128)(2,1)}, f32[2048,256]{1,0:T(8,128)}) fusion(f32[256,8,2,128]{3,2,1,0:T(2,128)S(1)} %bitcast.809, f32[8,256]{1,0:T(8,128)S(1)} %copy-done.155, f32[16,256]{1,0:T(8,128)S(1)} %bitcast.924, f32[32,256]{1,0:T(8,128)S(1)} %bitcast.919, ...), kind=kOutput, calls=%fused_computation.45 | convolution fusion | flops 2154823680 | bytes 24633344 | tf_op jit(solution)/shard_map/dot_general | solution.py:171
  273.0 8.2 fusion.256
  297.5 4.7 div.301
  303.6 3.3 reshape.1603
  306.9 4.8 reduce_sum.113
  316.9 7.6 copy.1296
  324.5 4.1 add_divide_fusion
  331.6 3.5 reshape.1610
  335.1 3.6 div.302
  338.7 7.9 convert_reduce_fusion
  346.6 3.7 reduce.36
  354.7 3.1 reduce.40
  377.3 5.0 collective-permute-start.21
  437.2 3.7 div.308
  466.6 3.1 copy.1123
  476.1 3.0 copy.1133
  482.2 7.1 fusion.258
  507.1 5.2 fusion.17
  512.3 145.0 %all-reduce.1 = bf16[256,2048]{1,0:T(8,128)(2,1)} all-reduce(f32[256,2048]{1,0:T(8,128)} %fusion.258), channel_id=1, replica_groups=mesh['seq'=32,'head'=8] {'seq'}, use_global_device_ids=true, to_apply=%region_12.13 | all-reduce | flops 524288 | bytes 3145728 | tf_op jit(solution)/shard_map/psum | solution.py:179
  659.8 3.0 copy.1210
  669.1 3.1 copy.1205
  673.8 3.2 copy.1197
  679.7 4.2 copy.1200
  685.6 4.5 copy.1146
  690.1 4.2 reshape_broadcast_in_dim_reshape_reshape.6
  700.1 3.0 copy.1154
  706.0 3.0 copy.1159
  719.7 7.6 collective-permute-start.26
  729.0 5.0 collective-permute-done.26
  734.4 3.0 collective-permute-start.27
  738.0 6.6 collective-permute-done.27
  745.0 12.7 %collective-permute-start.24 = (f32[2,16,256]{2,1,0:T(8,128)S(1)}, f32[2,16,256]{2,1,0:T(8,128)S(1)}, u32[]{:S(2)}, u32[]{:S(2)}) collective-permute-start(f32[2,16,256]{2,1,0:T(8,128)S(1)} %select_add_fusion.9), channel_id=1, source_target_pairs={{0,64},{64,0},{8,72},{72,8},{16,80},{80,16},{24,88},{88,24},{32,96... | collective-permute-start | bytes 98312 | tf_op jit(solution)/shard_map/ppermute | solution.py:17
  757.9 11.9 %collective-permute-start.29 = (f32[2,8,256]{1,2,0:T(8,128)S(1)}, f32[2,8,256]{1,2,0:T(8,128)S(1)}, u32[]{:S(2)}, u32[]{:S(2)}) collective-permute-start(f32[2,8,256]{1,2,0:T(8,128)S(1)} %select_add_fusion), channel_id=1, source_target_pairs={{0,128},{128,0},{8,136},{136,8},{16,144},{144,16},{24,152},{152,24... | collective-permute-start | bytes 49160 | tf_op jit(solution)/shard_map/ppermute | solution.py:17
  784.5 7.6 fusion.1
  802.0 7.6 fusion.9
  (826 shorter events, 422.3 us)
Async XLA Ops:
  7.2 253.6 %copy-start = (bf16[256,2048]{1,0:T(8,128)(2,1)S(1)}, bf16[256,2048]{1,0:T(8,128)(2,1)}, u32[]{:S(2)}) copy-start(bf16[256,2048]{1,0:T(8,128)(2,1)} %param.8) | copy-start | bytes 3145732
  7.2 247.9 %all-gather.2.cloned.1.call-start = ((), (), s32[]{:S(2)}) async-start(), calls=%async_computation.2 | async-start | bytes 9437184 | tf_op jit(solution)/shard_map/all_gather | solution.py:170
  40.1 140.7 %collective-permute-start.3 = (bf16[2,32,256]{2,1,0:T(8,128)(2,1)}, bf16[2,32,256]{2,1,0:T(8,128)(2,1)}, u32[]{:S(2)}, u32[]{:S(2)}) collective-permute-start(bf16[2,32,256]{2,1,0:T(8,128)(2,1)} %pad_maximum_fusion.7), channel_id=1, source_target_pairs={{0,8},{8,0},{16,24},{24,16},{32,40},{40,32},{48,56},{56,48},{64,72... | collective-permute-start | bytes 98312 | tf_op jit(solution)/shard_map/ppermute | solution.py:17
  43.6 128.5 %collective-permute-start.6 = (bf16[2,16,256]{2,1,0:T(8,128)(2,1)}, bf16[2,16,256]{2,1,0:T(8,128)(2,1)}, u32[]{:S(2)}, u32[]{:S(2)}) collective-permute-start(bf16[2,16,256]{2,1,0:T(8,128)(2,1)} %pad_maximum_fusion.8), channel_id=1, source_target_pairs={{0,8},{8,0},{16,24},{24,16},{32,40},{40,32},{48,56},{56,48},{64,72... | collective-permute-start | bytes 49160 | tf_op jit(solution)/shard_map/ppermute | solution.py:17
  43.8 767.1 %reduce-scatter.2.cloned.1.call-start = ((), (), s32[]{:S(2)}) async-start(), calls=%async_computation.1 | async-start | bytes 18874368 | tf_op jit(solution)/shard_map/reduce_scatter | solution.py:163
  44.5 123.5 %collective-permute-start.10 = (bf16[2,8,256]{2,1,0:T(8,128)(2,1)}, bf16[2,8,256]{2,1,0:T(8,128)(2,1)}, u32[]{:S(2)}, u32[]{:S(2)}) collective-permute-start(bf16[2,8,256]{2,1,0:T(8,128)(2,1)} %pad_maximum_fusion.9), channel_id=1, source_target_pairs={{0,8},{8,0},{16,24},{24,16},{32,40},{40,32},{48,56},{56,48},{64,72... | collective-permute-start | bytes 24584 | tf_op jit(solution)/shard_map/ppermute | solution.py:17
  47.2 138.1 %collective-permute-start.1 = (bf16[2,64,256]{2,1,0:T(8,128)(2,1)}, bf16[2,64,256]{2,1,0:T(8,128)(2,1)}, u32[]{:S(2)}, u32[]{:S(2)}) collective-permute-start(bf16[2,64,256]{2,1,0:T(8,128)(2,1)} %pad_maximum_fusion.6), channel_id=1, source_target_pairs={{0,8},{8,0},{16,24},{24,16},{32,40},{40,32},{48,56},{56,48},{64,72... | collective-permute-start | bytes 196616 | tf_op jit(solution)/shard_map/ppermute | solution.py:17
  47.9 151.5 %collective-permute-start = (bf16[2,128,256]{2,1,0:T(8,128)(2,1)}, bf16[2,128,256]{2,1,0:T(8,128)(2,1)}, u32[]{:S(2)}, u32[]{:S(2)}) collective-permute-start(bf16[2,128,256]{2,1,0:T(8,128)(2,1)} %pad_maximum_fusion.5), channel_id=1, source_target_pairs={{0,8},{8,0},{16,24},{24,16},{32,40},{40,32},{48,56},{56,48},{64,72... | collective-permute-start | bytes 393224 | tf_op jit(solution)/shard_map/ppermute | solution.py:17
  53.2 73.6 %copy-start.4 = (bf16[16,128,2,128]{3,2,1,0:T(2,128)(2,1)}, bf16[16,128,2,128]{3,2,1,0:T(2,128)(2,1)S(1)}, u32[]{:S(2)}) copy-start(bf16[16,128,2,128]{3,2,1,0:T(2,128)(2,1)S(1)} %reshape.1565) | copy-start | bytes 3145732
  81.8 49.9 %copy-start.92 = (bf16[2,128,2,128]{1,3,2,0:T(8,128)(2,1)}, bf16[2,128,2,128]{1,3,2,0:T(8,128)(2,1)S(1)}, u32[]{:S(2)}) copy-start(bf16[2,128,2,128]{1,3,2,0:T(8,128)(2,1)S(1)} %copy.1113) | copy-start | bytes 393220
  81.8 13.4 %copy-start.59 = (bf16[8,2,128,2,128]{4,3,2,1,0:T(2,128)(2,1)S(1)}, bf16[8,2,128,2,128]{4,3,2,1,0:T(2,128)(2,1)}, u32[]{:S(2)}) copy-start(bf16[8,2,128,2,128]{4,3,2,1,0:T(2,128)(2,1)} %reshape_reshape.4) | copy-start | bytes 3145732
  86.3 35.7 %copy-start.67 = (bf16[4,128,2,128]{1,3,2,0:T(8,128)(2,1)}, bf16[4,128,2,128]{1,3,2,0:T(8,128)(2,1)S(1)}, u32[]{:S(2)}) copy-start(bf16[4,128,2,128]{1,3,2,0:T(8,128)(2,1)S(1)} %copy.1155) | copy-start | bytes 786436
  98.4 28.5 %copy-start.23 = (bf16[8,2,128,2,128]{4,2,3,1,0:T(8,128)(2,1)}, bf16[8,2,128,2,128]{4,2,3,1,0:T(8,128)(2,1)S(1)}, u32[]{:S(2)}) copy-start(bf16[8,2,128,2,128]{4,2,3,1,0:T(8,128)(2,1)S(1)} %copy.995) | copy-start | bytes 3145732
  164.2 16.6 %copy-start.134 = (bf16[1,32,256]{2,1,0:T(8,128)(2,1)S(1)}, bf16[1,32,256]{2,1,0:T(8,128)(2,1)}, u32[]{:S(2)}) copy-start(bf16[1,32,256]{2,1,0:T(8,128)(2,1)} %copy-done.133) | copy-start | bytes 49156
  164.2 16.6 %copy-start.136 = (bf16[1,32,256]{2,1,0:T(8,128)(2,1)S(1)}, bf16[1,32,256]{2,1,0:T(8,128)(2,1)}, u32[]{:S(2)}) copy-start(bf16[1,32,256]{2,1,0:T(8,128)(2,1)} %copy-done.135) | copy-start | bytes 49156
  164.2 21.0 %copy-start.120 = (bf16[1,64,256]{2,1,0:T(8,128)(2,1)S(1)}, bf16[1,64,256]{2,1,0:T(8,128)(2,1)}, u32[]{:S(2)}) copy-start(bf16[1,64,256]{2,1,0:T(8,128)(2,1)} %copy-done.119) | copy-start | bytes 98308
  164.2 21.0 %copy-start.122 = (bf16[1,64,256]{2,1,0:T(8,128)(2,1)S(1)}, bf16[1,64,256]{2,1,0:T(8,128)(2,1)}, u32[]{:S(2)}) copy-start(bf16[1,64,256]{2,1,0:T(8,128)(2,1)} %copy-done.121) | copy-start | bytes 98308
  168.8 5.1 collective-permute-start.11
  173.0 9.5 %collective-permute-start.7 = (bf16[2,32,256]{2,1,0:T(8,128)(2,1)S(1)}, bf16[2,32,256]{2,1,0:T(8,128)(2,1)S(1)}, u32[]{:S(2)}, u32[]{:S(2)}) collective-permute-start(bf16[2,32,256]{2,1,0:T(8,128)(2,1)S(1)} %maximum_select_fusion.7), channel_id=1, source_target_pairs={{0,16},{16,0},{8,24},{24,8},{32,48},{48,32},{40,56},{56,40},{64,80... | collective-permute-start | bytes 98312 | tf_op jit(solution)/shard_map/ppermute | solution.py:17
  173.9 10.0 %collective-permute-start.12 = (bf16[2,32,256]{2,1,0:T(8,128)(2,1)S(1)}, bf16[2,32,256]{2,1,0:T(8,128)(2,1)S(1)}, u32[]{:S(2)}, u32[]{:S(2)}) collective-permute-start(bf16[2,32,256]{2,1,0:T(8,128)(2,1)S(1)} %maximum_select_fusion.8), channel_id=1, source_target_pairs={{0,32},{32,0},{8,40},{40,8},{16,48},{48,16},{24,56},{56,24},{64,96... | collective-permute-start | bytes 98312 | tf_op jit(solution)/shard_map/ppermute | solution.py:17
  181.7 9.0 %collective-permute-start.4 = (bf16[2,64,256]{2,1,0:T(8,128)(2,1)S(1)}, bf16[2,64,256]{2,1,0:T(8,128)(2,1)S(1)}, u32[]{:S(2)}, u32[]{:S(2)}) collective-permute-start(bf16[2,64,256]{2,1,0:T(8,128)(2,1)S(1)} %maximum_select_fusion.4), channel_id=1, source_target_pairs={{0,16},{16,0},{8,24},{24,8},{32,48},{48,32},{40,56},{56,40},{64,80... | collective-permute-start | bytes 196616 | tf_op jit(solution)/shard_map/ppermute | solution.py:17
  182.6 11.9 %collective-permute-start.8 = (bf16[2,64,256]{2,1,0:T(8,128)(2,1)S(1)}, bf16[2,64,256]{2,1,0:T(8,128)(2,1)S(1)}, u32[]{:S(2)}, u32[]{:S(2)}) collective-permute-start(bf16[2,64,256]{2,1,0:T(8,128)(2,1)S(1)} %maximum_select_fusion.5), channel_id=1, source_target_pairs={{0,32},{32,0},{8,40},{40,8},{16,48},{48,16},{24,56},{56,24},{64,96... | collective-permute-start | bytes 196616 | tf_op jit(solution)/shard_map/ppermute | solution.py:17
  183.9 12.0 %collective-permute-start.13 = (bf16[2,64,256]{2,1,0:T(8,128)(2,1)S(1)}, bf16[2,64,256]{2,1,0:T(8,128)(2,1)S(1)}, u32[]{:S(2)}, u32[]{:S(2)}) collective-permute-start(bf16[2,64,256]{2,1,0:T(8,128)(2,1)S(1)} %maximum_select_fusion.6), channel_id=1, source_target_pairs={{0,64},{64,0},{8,72},{72,8},{16,80},{80,16},{24,88},{88,24},{32,96... | collective-permute-start | bytes 196616 | tf_op jit(solution)/shard_map/ppermute | solution.py:17
  186.8 25.5 %collective-permute-start.2 = (bf16[2,128,256]{2,1,0:T(8,128)(2,1)}, bf16[2,128,256]{2,1,0:T(8,128)(2,1)}, u32[]{:S(2)}, u32[]{:S(2)}) collective-permute-start(bf16[2,128,256]{2,1,0:T(8,128)(2,1)} %maximum_select_fusion), channel_id=1, source_target_pairs={{0,16},{16,0},{8,24},{24,8},{32,48},{48,32},{40,56},{56,40},{64,80... | collective-permute-start | bytes 393224 | tf_op jit(solution)/shard_map/ppermute | solution.py:17
  191.3 31.8 %collective-permute-start.5 = (bf16[2,128,256]{2,1,0:T(8,128)(2,1)}, bf16[2,128,256]{2,1,0:T(8,128)(2,1)}, u32[]{:S(2)}, u32[]{:S(2)}) collective-permute-start(bf16[2,128,256]{2,1,0:T(8,128)(2,1)} %maximum_select_fusion.1), channel_id=1, source_target_pairs={{0,32},{32,0},{8,40},{40,8},{16,48},{48,16},{24,56},{56,24},{64,96... | collective-permute-start | bytes 393224 | tf_op jit(solution)/shard_map/ppermute | solution.py:17
  195.2 38.7 %collective-permute-start.9 = (bf16[2,128,256]{2,1,0:T(8,128)(2,1)}, bf16[2,128,256]{2,1,0:T(8,128)(2,1)}, u32[]{:S(2)}, u32[]{:S(2)}) collective-permute-start(bf16[2,128,256]{2,1,0:T(8,128)(2,1)} %maximum_select_fusion.2), channel_id=1, source_target_pairs={{0,64},{64,0},{8,72},{72,8},{16,80},{80,16},{24,88},{88,24},{32,96... | collective-permute-start | bytes 393224 | tf_op jit(solution)/shard_map/ppermute | solution.py:17
  196.5 46.4 %collective-permute-start.14 = (bf16[2,128,256]{2,1,0:T(8,128)(2,1)}, bf16[2,128,256]{2,1,0:T(8,128)(2,1)}, u32[]{:S(2)}, u32[]{:S(2)}) collective-permute-start(bf16[2,128,256]{2,1,0:T(8,128)(2,1)} %maximum_select_fusion.3), channel_id=1, source_target_pairs={{0,128},{128,0},{8,136},{136,8},{16,144},{144,16},{24,152},{152,24... | collective-permute-start | bytes 393224 | tf_op jit(solution)/shard_map/ppermute | solution.py:17
  366.4 407.7 %collective-permute-start.15 = (f32[2,128,256]{1,2,0:T(8,128)}, f32[2,128,256]{1,2,0:T(8,128)}, u32[]{:S(2)}, u32[]{:S(2)}) collective-permute-start(f32[2,128,256]{1,2,0:T(8,128)} %pad_maximum_fusion.1), channel_id=1, source_target_pairs={{0,8},{8,0},{16,24},{24,16},{32,40},{40,32},{48,56},{56,48},{64,72... | collective-permute-start | bytes 786440 | tf_op jit(solution)/shard_map/ppermute | solution.py:17
  369.3 13.8 %copy-start.124 = (bf16[1,128,256]{1,2,0:T(8,128)(2,1)S(1)}, bf16[1,128,256]{1,2,0:T(8,128)(2,1)}, u32[]{:S(2)}) copy-start(bf16[1,128,256]{1,2,0:T(8,128)(2,1)} %copy.1068) | copy-start | bytes 196612
  369.3 13.8 %copy-start.143 = (f32[2,8,128]{2,1,0:T(8,128)S(1)}, f32[2,8,128]{2,1,0:T(8,128)}, u32[]{:S(2)}) copy-start(f32[2,8,128]{2,1,0:T(8,128)} %get-tuple-element.122) | copy-start | bytes 24580
  369.3 13.9 %copy-start.144 = (f32[8,1,256]{2,1,0:T(1,128)S(1)}, f32[8,1,256]{2,1,0:T(1,128)}, u32[]{:S(2)}) copy-start(f32[8,1,256]{2,1,0:T(1,128)} %get-tuple-element.119) | copy-start | bytes 24580
  369.3 14.0 %copy-start.145 = (f32[8,1,256]{2,1,0:T(1,128)S(1)}, f32[8,1,256]{2,1,0:T(1,128)}, u32[]{:S(2)}) copy-start(f32[8,1,256]{2,1,0:T(1,128)} %get-tuple-element.120) | copy-start | bytes 24580
  369.3 342.9 %collective-permute-start.16 = (f32[2,64,256]{2,1,0:T(8,128)}, f32[2,64,256]{2,1,0:T(8,128)}, u32[]{:S(2)}, u32[]{:S(2)}) collective-permute-start(f32[2,64,256]{2,1,0:T(8,128)} %broadcast_select_fusion.2), channel_id=1, source_target_pairs={{0,8},{8,0},{16,24},{24,16},{32,40},{40,32},{48,56},{56,48},{64,72... | collective-permute-start | bytes 393224 | tf_op jit(solution)/shard_map/ppermute | solution.py:17
  373.6 341.3 %collective-permute-start.18 = (f32[2,64,256]{2,1,0:T(8,128)}, f32[2,64,256]{2,1,0:T(8,128)}, u32[]{:S(2)}, u32[]{:S(2)}) collective-permute-start(f32[2,64,256]{2,1,0:T(8,128)} %broadcast_select_fusion.1), channel_id=1, source_target_pairs={{0,16},{16,0},{8,24},{24,8},{32,48},{48,32},{40,56},{56,40},{64,80... | collective-permute-start | bytes 393224 | tf_op jit(solution)/shard_map/ppermute | solution.py:17
  374.6 14.8 %copy-start.38 = (f32[4,2,128,128]{2,3,1,0:T(8,128)S(1)}, f32[4,2,128,128]{2,3,1,0:T(8,128)}, u32[]{:S(2)}) copy-start(f32[4,2,128,128]{2,3,1,0:T(8,128)} %copy-done.37) | copy-start | bytes 1572868
  377.3 338.7 %collective-permute-start.21 = (f32[2,64,256]{2,1,0:T(8,128)}, f32[2,64,256]{2,1,0:T(8,128)}, u32[]{:S(2)}, u32[]{:S(2)}) collective-permute-start(f32[2,64,256]{2,1,0:T(8,128)} %broadcast_select_fusion), channel_id=1, source_target_pairs={{0,32},{32,0},{8,40},{40,8},{16,48},{48,16},{24,56},{56,24},{64,96... | collective-permute-start | bytes 393224 | tf_op jit(solution)/shard_map/ppermute | solution.py:17
  385.8 332.7 %collective-permute-start.25 = (f32[2,64,256]{1,2,0:T(8,128)}, f32[2,64,256]{1,2,0:T(8,128)}, u32[]{:S(2)}, u32[]{:S(2)}) collective-permute-start(f32[2,64,256]{1,2,0:T(8,128)} %fusion.109), channel_id=1, source_target_pairs={{0,64},{64,0},{8,72},{72,8},{16,80},{80,16},{24,88},{88,24},{32,96... | collective-permute-start | bytes 393224 | tf_op jit(solution)/shard_map/ppermute | solution.py:17
  512.3 145.0 %copy-start.69 = (f32[2,2,128,2,128]{4,3,2,1,0:T(2,128)S(1)}, f32[2,2,128,2,128]{4,3,2,1,0:T(2,128)}, u32[]{:S(2)}) copy-start(f32[2,2,128,2,128]{4,3,2,1,0:T(2,128)} %copy.1209) | copy-start | bytes 1572868
  713.1 62.0 %collective-permute-start.17 = (f32[2,64,256]{2,1,0:T(8,128)S(1)}, f32[2,64,256]{2,1,0:T(8,128)S(1)}, u32[]{:S(2)}, u32[]{:S(2)}) collective-permute-start(f32[2,64,256]{2,1,0:T(8,128)S(1)} %select_add_fusion.6), channel_id=1, source_target_pairs={{0,16},{16,0},{8,24},{24,8},{32,48},{48,32},{40,56},{56,40},{64,80... | collective-permute-start | bytes 393224 | tf_op jit(solution)/shard_map/ppermute | solution.py:17
  715.9 11.5 %collective-permute-start.19 = (f32[2,32,256]{2,1,0:T(8,128)S(1)}, f32[2,32,256]{2,1,0:T(8,128)S(1)}, u32[]{:S(2)}, u32[]{:S(2)}) collective-permute-start(f32[2,32,256]{2,1,0:T(8,128)S(1)} %slice_select_fusion.4), channel_id=1, source_target_pairs={{0,8},{8,0},{16,24},{24,16},{32,40},{40,32},{48,56},{56,48},{64,72... | collective-permute-start | bytes 196616 | tf_op jit(solution)/shard_map/ppermute | solution.py:17
  717.0 20.5 %collective-permute-start.22 = (f32[2,32,256]{2,1,0:T(8,128)S(1)}, f32[2,32,256]{2,1,0:T(8,128)S(1)}, u32[]{:S(2)}, u32[]{:S(2)}) collective-permute-start(f32[2,32,256]{2,1,0:T(8,128)S(1)} %slice_select_fusion.3), channel_id=1, source_target_pairs={{0,16},{16,0},{8,24},{24,8},{32,48},{48,32},{40,56},{56,40},{64,80... | collective-permute-start | bytes 196616 | tf_op jit(solution)/shard_map/ppermute | solution.py:17
  719.7 14.3 %collective-permute-start.26 = (f32[2,32,256]{1,2,0:T(8,128)S(1)}, f32[2,32,256]{1,2,0:T(8,128)S(1)}, u32[]{:S(2)}, u32[]{:S(2)}) collective-permute-start(f32[2,32,256]{1,2,0:T(8,128)S(1)} %slice_select_fusion.2), channel_id=1, source_target_pairs={{0,32},{32,0},{8,40},{40,8},{16,48},{48,16},{24,56},{56,24},{64,96... | collective-permute-start | bytes 196616 | tf_op jit(solution)/shard_map/ppermute | solution.py:17
  727.4 42.4 %collective-permute-start.20 = (f32[2,32,256]{2,1,0:T(8,128)S(1)}, f32[2,32,256]{2,1,0:T(8,128)S(1)}, u32[]{:S(2)}, u32[]{:S(2)}) collective-permute-start(f32[2,32,256]{2,1,0:T(8,128)S(1)} %select_add_fusion.8), channel_id=1, source_target_pairs={{0,32},{32,0},{8,40},{40,8},{16,48},{48,16},{24,56},{56,24},{64,96... | collective-permute-start | bytes 196616 | tf_op jit(solution)/shard_map/ppermute | solution.py:17
  734.4 10.2 %collective-permute-start.27 = (f32[2,16,256]{1,2,0:T(8,128)S(1)}, f32[2,16,256]{1,2,0:T(8,128)S(1)}, u32[]{:S(2)}, u32[]{:S(2)}) collective-permute-start(f32[2,16,256]{1,2,0:T(8,128)S(1)} %slice_select_fusion.1), channel_id=1, source_target_pairs={{0,16},{16,0},{8,24},{24,8},{32,48},{48,32},{40,56},{56,40},{64,80... | collective-permute-start | bytes 98312 | tf_op jit(solution)/shard_map/ppermute | solution.py:17
  737.4 7.6 collective-permute-start.23
  744.8 12.9 %collective-permute-start.28 = (f32[2,8,256]{1,2,0:T(8,128)S(1)}, f32[2,8,256]{1,2,0:T(8,128)S(1)}, u32[]{:S(2)}, u32[]{:S(2)}) collective-permute-start(f32[2,8,256]{1,2,0:T(8,128)S(1)} %slice_select_fusion), channel_id=1, source_target_pairs={{0,8},{8,0},{16,24},{24,16},{32,40},{40,32},{48,56},{56,48},{64,72... | collective-permute-start | bytes 49160 | tf_op jit(solution)/shard_map/ppermute | solution.py:17
  745.0 26.9 %collective-permute-start.24 = (f32[2,16,256]{2,1,0:T(8,128)S(1)}, f32[2,16,256]{2,1,0:T(8,128)S(1)}, u32[]{:S(2)}, u32[]{:S(2)}) collective-permute-start(f32[2,16,256]{2,1,0:T(8,128)S(1)} %select_add_fusion.9), channel_id=1, source_target_pairs={{0,64},{64,0},{8,72},{72,8},{16,80},{80,16},{24,88},{88,24},{32,96... | collective-permute-start | bytes 98312 | tf_op jit(solution)/shard_map/ppermute | solution.py:17
  757.9 22.0 %collective-permute-start.29 = (f32[2,8,256]{1,2,0:T(8,128)S(1)}, f32[2,8,256]{1,2,0:T(8,128)S(1)}, u32[]{:S(2)}, u32[]{:S(2)}) collective-permute-start(f32[2,8,256]{1,2,0:T(8,128)S(1)} %select_add_fusion), channel_id=1, source_target_pairs={{0,128},{128,0},{8,136},{136,8},{16,144},{144,16},{24,152},{152,24... | collective-permute-start | bytes 49160 | tf_op jit(solution)/shard_map/ppermute | solution.py:17
  (157 other events, 689.5 us)
Sparse Core Ops, SparseCore 0:
  43.9 55.0 all-gather.1
  281.3 95.7 reduce-scatter.1
where the time goes:
time: 833 us; the launch traced here: 821 us
  local copies, waits for them, and re-layouts  371 us (45%)
  blocking collectives  145 us (17%)
  other arithmetic  111 us (13%)
  matrix products  84.4 us (10%)
  starting transfers between devices  77.5 us (9%)
  between operations  16.9 us (2%)
  waiting for transfers between devices  15.2 us (2%)
    psum x1, blocking collectives, body(): grad_weight = lax.psum(grad_proj, 'seq').astype(jnp.bfloat16)  145 us
    ppermute x30, starting transfers between devices, from_partner(): return lax.ppermute(block, axis, route)  77.4 us
    broadcast_in_dim x45, local copies, waits for them, and re-layouts, spread(): jnp.broadcast_to(matrix[:, None], (dims_in[0], repeats) + dims_in[1:])  37.9 us
    unnamed x378, local copies, waits for them, and re-layouts  36.3 us
    div x17, local copies, waits for them, and re-layouts, body(): grad_q = grad_q + spread(as_rows(level_q), 2 ** level) / weight  31.7 us
    rev x12, local copies, waits for them, and re-layouts, swap_blocks(): blocks.reshape((dims_in[0] // 2, 2) + dims_in[1:])[:, ::-1].reshape(dims_in)  27.6 us
    reshape x14, local copies, waits for them, and re-layouts, spread(): return widened.reshape((dims_in[0] * repeats,) + dims_in[1:])  26.1 us
    convert_element_type x16, local copies, waits for them, and re-layouts, pair_mean(): return ((pairs[..., 0, :] + pairs[..., 1, :]) * 0.5).astype(jnp.bfloat16)  26.1 us
  transfers between devices with their start and end apart: 32, of which 4 were waited for; matrix products, arithmetic and copies ran while one was open for 60% of the time, Pallas kernels for 0%

commit v1 on v0

v1 whole, which is shorter than its diff:
```python
import functools
import jax
import jax.numpy as jnp
from jax import lax
from jax.experimental import pallas as pl
from jax.experimental.pallas import tpu as pltpu
from jax.sharding import PartitionSpec as P

HD = 128
B = 128
LOCAL = 4
F32 = jnp.float32
BF16 = jnp.bfloat16
EXP_SCALE = 1.4426950408889634 * HD ** (-0.5)
SCALE = HD ** (-0.5)
VMEM = 56 * 1024 * 1024


def nn(a, b):
    return lax.dot_general(a, b, (((1,), (0,)), ((), ())), preferred_element_type=F32)


def nt(a, b):
    return lax.dot_general(a, b, (((1,), (1,)), ((), ())), preferred_element_type=F32)


def tn(a, b):
    return lax.dot_general(a, b, (((0,), (0,)), ((), ())), preferred_element_type=F32)


def params():
    return pltpu.CompilerParams(vmem_limit_bytes=VMEM)


def offset(level, tokens):
    return tokens - (tokens >> (level - 1))


def spec(rows, block=0):
    return pl.BlockSpec((rows, HD), lambda h: (block, h))


def lead(rows, width):
    return pl.BlockSpec((1, rows, width), lambda h: (h, 0, 0))


def with_ones(v):
    return jnp.concatenate([v, jnp.ones(v.shape, BF16)], axis=1)


def repeat2(x, scratch, base=0):
    n = x.shape[0]
    scratch[pl.ds(base, n, stride=2), :] = x
    scratch[pl.ds(base + 1, n, stride=2), :] = x


def coarsen_kernel(q_ref, k_ref, v_ref, qc_ref, kc_ref, vc_ref):
    tokens = q_ref.shape[0]
    r = lax.broadcasted_iota(jnp.int32, (B, 2 * B), 0)
    c = lax.broadcasted_iota(jnp.int32, (B, 2 * B), 1)
    mean = jnp.where(c // 2 == r, 0.5, 0.0).astype(BF16)
    half = mean[:64, :128]
    for src, dst in ((q_ref, qc_ref), (k_ref, kc_ref), (v_ref, vc_ref)):
        for i in range(tokens // 256):
            dst[i * B:(i + 1) * B, :] = nn(mean, src[i * 256:(i + 1) * 256, :]).astype(BF16)
    for level in range(2, LOCAL + 1):
        before, here = offset(level - 1, tokens), offset(level, tokens)
        for dst in (qc_ref, kc_ref, vc_ref):
            for i in range((tokens >> level) // B):
                rows = dst[before + i * 256:before + (i + 1) * 256, :]
                dst[here + i * B:here + (i + 1) * B, :] = nn(mean, rows).astype(BF16)
    tail = offset(LOCAL + 1, tokens)
    for dst in (qc_ref, kc_ref, vc_ref):
        x5 = nn(half, dst[tail - B:tail, :]).astype(BF16)
        x6 = nn(half[:32, :64], x5).astype(BF16)
        x7 = nn(half[:16, :32], x6).astype(BF16)
        x8 = nn(half[:16, :16], x7).astype(BF16)
        dst[tail:tail + 64, :] = x5
        dst[tail + 64:tail + 96, :] = x6
        dst[tail + 96:tail + 112, :] = x7
        dst[tail + 112:tail + 128, :] = x8


def coarsen(q, k, v):
    shape = jax.ShapeDtypeStruct(q.shape, BF16)
    tokens = q.shape[0]
    return pl.pallas_call(
        coarsen_kernel,
        grid=(q.shape[1] // HD,),
        in_specs=[spec(tokens)] * 3,
        out_specs=[spec(tokens)] * 3,
        out_shape=[shape] * 3,
        compiler_params=params(),
        name="coarsen",
    )(q, k, v)


def forward_block(q, k, v):
    expos = jnp.exp2(nt(q, k) * EXP_SCALE).astype(BF16)
    return nn(expos, with_ones(v))


def local_forward_kernel(q_ref, k_ref, v_ref, qc_ref, kc_ref, vc_ref, numer_ref, total_ref, *scr):
    tokens = q_ref.shape[0]
    for level in range(LOCAL - 1, 0, -1):
        off = offset(level, tokens)
        for i in range((tokens >> level) // 256):
            at = off + i * 256
            lo, hi = slice(at, at + B), slice(at + B, at + 256)
            for j, (mine, other) in enumerate(((lo, hi), (hi, lo))):
                u = forward_block(qc_ref[mine, :], kc_ref[other, :], vc_ref[other, :])
                n, t = u[:, :HD], u[:, HD:]
                rows = slice(i * 256 + j * B, i * 256 + (j + 1) * B)
                if level < LOCAL - 1:
                    n = n + 2.0 * scr[2 * level][rows, :]
                    t = t + 2.0 * scr[2 * level + 1][rows, :]
                repeat2(n, scr[2 * level - 2], 2 * rows.start)
                repeat2(t, scr[2 * level - 1], 2 * rows.start)
    for i in range(tokens // 256):
        rows = slice(i * 256, (i + 1) * 256)
        u = forward_block(q_ref[rows, :], k_ref[rows, :], v_ref[rows, :])
        numer_ref[0, rows, :] = u[:, :HD] + 2.0 * scr[0][rows, :]
        total_ref[0, rows, :] = u[:, HD:] + 2.0 * scr[1][rows, :]


def local_forward(q, k, v, qc, kc, vc):
    tokens, width = q.shape
    heads = width // HD
    scratch = []
    for level in range(1, LOCAL):
        scratch += [pltpu.VMEM((tokens >> (level - 1), HD), F32)] * 2
    shape = jax.ShapeDtypeStruct((heads, tokens, HD), F32)
    return pl.pallas_call(
        local_forward_kernel,
        grid=(heads,),
        in_specs=[spec(tokens)] * 6,
        out_specs=[lead(tokens, HD)] * 2,
        out_shape=[shape] * 2,
        scratch_shapes=scratch,
        compiler_params=params(),
        name="local_forward",
    )(q, k, v, qc, kc, vc)


def level_of_row(row):
    steps = [(row >= edge).astype(jnp.int32) for edge in (128, 192, 224, 240, 248)]
    return sum(steps)


def spread_levels(packed, scratch, weight):
    bounds = (0, 128, 192, 224, 240, 248)
    x = packed[240:248, :]
    for i in range(3, -1, -1):
        lo, hi = bounds[i], bounds[i + 1]
        repeat2(x, scratch)
        x = packed[lo:hi, :] + weight * scratch[0:hi - lo, :]
    return x


def repeat16(x, scratch):
    n = x.shape[0]
    for j in range(16):
        scratch[pl.ds(j, n, stride=16), :] = x


def coarse_forward_kernel(numer_ref, total_ref, q_ref, k_ref, v_ref, att_ref, rtot_ref, small, big_n, big_t):
    rows, keys = q_ref.shape[0], k_ref.shape[0]
    level = level_of_row(lax.broadcasted_iota(jnp.int32, (rows, keys), 0))
    group = lax.broadcasted_iota(jnp.int32, (rows, keys), 1) // B
    expos = jnp.where(level == group, jnp.exp2(nt(q_ref[...], k_ref[...]) * EXP_SCALE), 0.0)
    u = nn(expos.astype(BF16), with_ones(v_ref[...]))
    repeat16(16.0 * spread_levels(u[:, :HD], small, 2.0), big_n)
    repeat16(16.0 * spread_levels(u[:, HD:], small, 2.0), big_t)
    rtot = 1.0 / (total_ref[0] + big_t[...])
    rtot_ref[0] = rtot
    att_ref[...] = ((numer_ref[0] + big_n[...]) * rtot).astype(BF16)


def coarse_forward(numer, total, qc, kall, vall):
    heads, tokens, _ = numer.shape
    keys = kall.shape[0]
    return pl.pallas_call(
        coarse_forward_kernel,
        grid=(heads,),
        in_specs=[lead(tokens, HD)] * 2 + [spec(256, tokens // 256 - 1)] + [spec(keys)] * 2,
        out_specs=[spec(tokens), lead(tokens, HD)],
        out_shape=[
            jax.ShapeDtypeStruct((tokens, heads * HD), BF16),
            jax.ShapeDtypeStruct((heads, tokens, HD), F32),
        ],
        scratch_shapes=[pltpu.VMEM((B, HD), F32)] + [pltpu.VMEM((tokens, HD), F32)] * 2,
        compiler_params=params(),
        name="coarse_forward",
    )(numer, total, qc, kall, vall)


def with_dot(g, dot):
    lane = lax.broadcasted_iota(jnp.int32, dot.shape, 1)
    high = (-dot).astype(BF16)
    low = (-dot - high.astype(F32)).astype(BF16)
    zero = jnp.zeros(dot.shape, BF16)
    parts = jnp.where(lane == 0, high, jnp.where(lane == 1, low, zero))
    return jnp.concatenate([g.astype(BF16), parts], axis=1)


def backward_block(q, k, v, g, mask=None):
    expos = jnp.exp2(nt(k, q) * EXP_SCALE)
    if mask is not None:
        expos = jnp.where(mask, expos, 0.0)
    slopes = (expos * nt(with_ones(v), g)).astype(BF16)
    dq = tn(slopes, k)
    dk = nn(slopes, q)
    dv = nn(expos.astype(BF16), g[:, :HD])
    return dq, dk, dv


def coarse_backward_kernel(
    ga_ref, att_ref, rtot_ref, q_ref, k_ref, v_ref, g0_ref, gc_ref, dq_ref, dk_ref, dv_ref, g_scr, d_scr, small
):
    tokens = ga_ref.shape[0]
    step = 256
    for i in range(tokens // step):
        rows = slice(i * step, (i + 1) * step)
        ga = ga_ref[rows, :].astype(F32)
        rtot = rtot_ref[0, rows, :]
        g = ga * rtot
        dot = jnp.sum(ga * att_ref[rows, :].astype(F32), axis=1, keepdims=True) * rtot
        g_scr[rows, :] = g
        d_scr[rows, :] = dot
        g0_ref[0, rows, :] = with_dot(g, dot)
    for level in range(1, 9):
        n = tokens >> level
        here = offset(level, tokens)
        chunk = min(n, 256)
        for i in range(n // chunk):
            even, odd = pl.ds(2 * i * chunk, chunk, stride=2), pl.ds(2 * i * chunk + 1, chunk, stride=2)
            g = g_scr[even, :] + g_scr[odd, :]
            dot = d_scr[even, :] + d_scr[odd, :]
            g_scr[i * chunk:(i + 1) * chunk, :] = g
            d_scr[i * chunk:(i + 1) * chunk, :] = dot
            if n < 16:
                pad = jnp.zeros((16 - n, HD), F32)
                g, dot = jnp.concatenate([g, pad], axis=0), jnp.concatenate([dot, pad], axis=0)
            gc_ref[0, here + i * chunk:here + i * chunk + g.shape[0], :] = with_dot(g, dot)
    rows, keys = q_ref.shape[0], k_ref.shape[0]
    level = level_of_row(lax.broadcasted_iota(jnp.int32, (keys, rows), 1))
    group = lax.broadcasted_iota(jnp.int32, (keys, rows), 0) // B
    g = gc_ref[0, tokens - rows:tokens, :]
    dq, dk, dv = backward_block(q_ref[...], k_ref[...], v_ref[...], g, level == group)
    dq_ref[0] = spread_levels(dq, small, 1.0)
    dk_ref[...] = (dk * SCALE).astype(BF16)
    dv_ref[...] = dv.astype(BF16)


def coarse_backward(ga, att, rtot, qc, kall, vall):
    heads, tokens, _ = rtot.shape
    keys = kall.shape[0]
    wide = jax.ShapeDtypeStruct((heads, tokens, 2 * HD), BF16)
    side = jax.ShapeDtypeStruct((keys, heads * HD), BF16)
    return pl.pallas_call(
        coarse_backward_kernel,
        grid=(heads,),
        in_specs=[spec(tokens)] * 2 + [lead(tokens, HD), spec(256, tokens // 256 - 1)] + [spec(keys)] * 2,
        out_specs=[lead(tokens, 2 * HD)] * 2 + [lead(B, HD)] + [spec(keys)] * 2,
        out_shape=[wide, wide, jax.ShapeDtypeStruct((heads, B, HD), F32), side, side],
        scratch_shapes=[pltpu.VMEM((tokens, HD), F32)] * 2 + [pltpu.VMEM((B, HD), F32)],
        compiler_params=params(),
        name="coarse_backward",
    )(ga, att, rtot, qc, kall, vall)


def local_backward_kernel(
    q_ref, k_ref, v_ref, qc_ref, kc_ref, vc_ref, g0_ref, gc_ref, dq4_ref, dq_ref, dk_ref, dv_ref, *scr
):
    tokens = q_ref.shape[0]
    for level in range(LOCAL - 1, 0, -1):
        off = offset(level, tokens)
        sq, sk, sv = scr[3 * level - 3:3 * level]
        if level == LOCAL - 1:
            repeat2(dq4_ref[0], scr[3 * level])
        uq = scr[3 * level]
        uk, uv = scr[3 * level + 1:3 * level + 3] if level < LOCAL - 1 else (None, None)
        for i in range((tokens >> level) // 256):
            at = off + i * 256
            lo, hi = (at, i * 256), (at + B, i * 256 + B)
            for (ma, mr), (oa, orow) in ((lo, hi), (hi, lo)):
                mine, other = slice(ma, ma + B), slice(oa, oa + B)
                dq, dk, dv = backward_block(qc_ref[mine, :], kc_ref[other, :], vc_ref[other, :], gc_ref[0, mine, :])
                dq = dq + uq[mr:mr + B, :]
                if uk is not None:
                    dk = dk + uk[orow:orow + B, :]
                    dv = dv + uv[orow:orow + B, :]
                repeat2(dq, sq, 2 * mr)
                repeat2(dk, sk, 2 * orow)
                repeat2(dv, sv, 2 * orow)
    for i in range(tokens // 256):
        rows = slice(i * 256, (i + 1) * 256)
        dq, dk, dv = backward_block(q_ref[rows, :], k_ref[rows, :], v_ref[rows, :], g0_ref[0, rows, :])
        dq_ref[rows, :] = ((dq + scr[0][rows, :]) * SCALE).astype(BF16)
        dk_ref[rows, :] = ((dk + scr[1][rows, :]) * SCALE).astype(BF16)
        dv_ref[rows, :] = (dv + scr[2][rows, :]).astype(BF16)


def local_backward(q, k, v, qc, kc, vc, g0, gc, dq4):
    tokens, width = q.shape
    heads = width // HD
    scratch = []
    for level in range(1, LOCAL):
        scratch += [pltpu.VMEM((tokens >> (level - 1), HD), F32)] * 3
    scratch += [pltpu.VMEM((tokens >> (LOCAL - 1), HD), F32)]
    shape = jax.ShapeDtypeStruct((tokens, width), BF16)
    return pl.pallas_call(
        local_backward_kernel,
        grid=(heads,),
        in_specs=[spec(tokens)] * 6 + [lead(tokens, 2 * HD)] * 2 + [lead(B, HD)],
        out_specs=[spec(tokens)] * 3,
        out_shape=[shape] * 3,
        scratch_shapes=scratch,
        compiler_params=params(),
        name="local_backward",
    )(q, k, v, qc, kc, vc, g0, gc, dq4)


def finish_kernel(dk_ref, dv_ref, ck_ref, cv_ref, gk_ref, gv_ref, small, big):
    for part, coarse, out in ((dk_ref, ck_ref, gk_ref), (dv_ref, cv_ref, gv_ref)):
        repeat16(spread_levels(coarse[...].astype(F32), small, 1.0), big)
        out[...] = (part[...].astype(F32) + big[...]).astype(BF16)


def finish(dk, dv, ck, cv):
    tokens, width = dk.shape
    shape = jax.ShapeDtypeStruct((tokens, width), BF16)
    return pl.pallas_call(
        finish_kernel,
        grid=(width // HD,),
        in_specs=[spec(tokens)] * 2 + [spec(256)] * 2,
        out_specs=[spec(tokens)] * 2,
        out_shape=[shape] * 2,
        scratch_shapes=[pltpu.VMEM((B, HD), F32), pltpu.VMEM((tokens, HD), F32)],
        compiler_params=params(),
        name="finish",
    )(dk, dv, ck, cv)


def swap(x, axis, distance):
    return lax.ppermute(x, axis, [(i, i ^ distance) for i in range(lax.axis_size(axis))])


ROWS = (128, 64, 32, 16, 8)
START = (0, 128, 192, 224, 240)


def cat(parts):
    return jnp.concatenate(parts, axis=0) if len(parts) > 1 else parts[0]


def gather_siblings(packed, count):
    groups = {i: packed[START[i]:START[i] + ROWS[i]] for i in range(count)}
    found = {}
    for b in range(0, count, 2):
        pair = b + 1 < count
        later = [i for i in range(b + 2, count)]
        common = [groups[i] for i in later]
        arrived = {}
        sent = {1: [groups[b]] + common}
        if pair:
            sent[2] = sent[3] = [groups[b + 1]] + common
        for j, parts in sent.items():
            arrived[j] = swap(cat(parts), "seq", j << b)
        found[b] = arrived[1][:B]
        if pair:
            found[b + 1] = cat([arrived[2][:64], arrived[3][:64]])
            lead = {1: B, 2: 64, 3: 64}
            for i in later:
                n = groups[i].shape[0]
                pieces = [groups[i]] + [arrived[j][lead[j]:lead[j] + n] for j in (1, 2, 3)]
                lead = {j: at + n for j, at in lead.items()}
                groups[i] = cat(pieces)
    return cat([found[i] for i in range(count)])


def return_siblings(partial, count):
    parts = {i: partial[i * B:(i + 1) * B] for i in range(count)}
    for b in range((count - 1) // 2 * 2, -1, -2):
        pair = b + 1 < count
        later = [i for i in range(b + 2, count)]
        quarter = {i: parts[i].shape[0] // 4 for i in later}
        cut = lambda i, j: parts[i][j * quarter[i]:(j + 1) * quarter[i]]
        sent = {1: [parts[b]] + [cut(i, 1) for i in later]}
        if pair:
            sent[2] = [parts[b + 1][:64]] + [cut(i, 2) for i in later]
            sent[3] = [parts[b + 1][64:]] + [cut(i, 3) for i in later]
        arrived = {j: swap(cat(x), "seq", j << b) for j, x in sent.items()}
        parts[b] = arrived[1][:B]
        if pair:
            parts[b + 1] = arrived[2][:64] + arrived[3][:64]
            lead = {1: B, 2: 64, 3: 64}
            for i in later:
                n = quarter[i]
                total = cut(i, 0).astype(F32)
                for j in (1, 2, 3):
                    total = total + arrived[j][lead[j]:lead[j] + n].astype(F32)
                lead = {j: at + n for j, at in lead.items()}
                parts[i] = total.astype(BF16)
    pad = jnp.zeros((256 - sum(ROWS[:count]), partial.shape[1]), partial.dtype)
    return cat([parts[i] for i in range(count)] + [pad])


def sum_over_sequence(x, count):
    low = max(count - 2, 0)
    n = x.shape[0] // 4
    high = lax.axis_index("seq") >> low
    if count < 2:
        for b in range(count):
            x = x + swap(x, "seq", 1 << b)
        return x.astype(BF16)
    pieces = lambda j: lax.dynamic_slice_in_dim(x, (high ^ j) * n, n, 0)
    arrived = [swap(pieces(j).astype(BF16), "seq", j << low) for j in (1, 2, 3)]
    total = pieces(0) + sum(y.astype(F32) for y in arrived)
    for b in range(low):
        mine = total.astype(BF16)
        total = total + swap(mine, "seq", 1 << b).astype(F32)
    mine = total.astype(BF16)
    whole = jnp.zeros(x.shape, BF16)
    for j, y in enumerate([mine] + [swap(mine, "seq", j << low) for j in (1, 2, 3)]):
        whole = lax.dynamic_update_slice_in_dim(whole, y, (high ^ j) * n, 0)
    return whole


def body(queries, keys, values, w_out, grad_out):
    tokens, width = queries.shape
    shards = lax.axis_size("head")
    count = lax.axis_size("seq").bit_length() - 1
    cotangent = lax.all_gather(grad_out, "head", axis=0, tiled=True)
    w_full = lax.all_gather(w_out, "head", axis=0, tiled=True)
    qc, kc, vc = coarsen(queries, keys, values)
    packed = jnp.concatenate([kc[tokens - 256:], vc[tokens - 256:]], axis=1)
    siblings = gather_siblings(packed, count)
    kall, vall = siblings[:, :width], siblings[:, width:]
    numer, total = local_forward(queries, keys, values, qc, kc, vc)
    attended, rtot = coarse_forward(numer, total, qc, kall, vall)

    mine = lax.all_to_all(attended.reshape(shards, tokens // shards, width), "head", 0, 0)
    mine = jnp.transpose(mine, (1, 0, 2)).reshape(tokens // shards, shards * width)
    mixed = jnp.dot(mine, w_full, preferred_element_type=F32).astype(BF16)
    ga = nt(cotangent, w_out)
    grad_weight = sum_over_sequence(tn(attended, cotangent), count)

    g0, gc, dq4, dk_side, dv_side = coarse_backward(ga, attended, rtot, qc, kall, vall)
    returned = return_siblings(jnp.concatenate([dk_side, dv_side], axis=1), count)
    grad_q, dk, dv = local_backward(queries, keys, values, qc, kc, vc, g0, gc, dq4)
    grad_k, grad_v = finish(dk, dv, returned[:, :width], returned[:, width:])
    return mixed, grad_q, grad_k, grad_v, grad_weight


def solution(mesh):
    return jax.shard_map(
        body,
        mesh=mesh,
        in_specs=(
            P("seq", "head"),
            P("seq", "head"),
            P("seq", "head"),
            P("head", None),
            P(("seq", "head"), None),
        ),
        out_specs=(
            P(("seq", "head"), None),
            P("seq", "head"),
            P("seq", "head"),
            P("seq", "head"),
            P("head", None),
        ),
        check_vma=False,
    )
```

time: 833 us -> 225 us (0.27)
  local copies, waits for them, and re-layouts: 371 us -> 10.2 us
  blocking collectives: 145 us -> 0 us
  other arithmetic: 111 us -> 1.79 us
  waiting for transfers between devices: 15.2 us -> 83.6 us
  matrix products: 84.4 us -> 16.4 us
  Pallas kernels: 0 us -> 48.3 us
  starting transfers between devices: 77.5 us -> 46.2 us
    psum x1 -> x0, blocking collectives: 145 us -> none  [body(): grad_weight = lax.psum(grad_proj, 'seq').astype(jnp.bfloat16)]
    div x44 -> x0, local copies, waits for them, and re-layouts: 85 us -> none  [the longest x17 31.7 us: body(): grad_q = grad_q + spread(as_rows(level_q), 2 ** level) / weight]
    dot_general x63 -> x3, matrix products: 84.4 us -> 16.4 us  [the longest x1 6.7 us: body(): mixed = jnp.dot(mine, w_full, preferred_element_type=F32).astype(BF16)]
    convert_element_type x39 -> x4, other arithmetic: 59.4 us -> 1.48 us  [the longest x3 1.46 us: sum_over_sequence(): mine = total.astype(BF16)]
    ppermute x30 -> x23, waiting for transfers between devices: 15.2 us -> 71.7 us  [swap(): lax.ppermute(x, axis, [(i, i ^ distance) for i in range(lax.axis_size(axi...]
    convert_element_type x47 -> x1, local copies, waits for them, and re-layouts: 49.8 us -> 1.04 us  [sum_over_sequence(): arrived = [swap(pieces(j).astype(BF16), 'seq', j << low) for j in (1, 2, 3)]]
    reshape x30 -> x1, local copies, waits for them, and re-layouts: 50.7 us -> 2.35 us  [body(): attended.reshape(shards, tokens // shards, width)]
    pallas_call x0 -> x6, Pallas kernels: none -> 48.3 us  [the longest x1 16.6 us: local_backward(): pl.pallas_call(local_backward_kernel, grid=(heads,), in_specs=[spec(token...]
  transfers between devices with their start and end apart: 32 -> 26, of which waited for: 4 -> 13; matrix products, arithmetic and copies ran while one was open for 60% -> 12% of each run, Pallas kernels for 0% -> 22%
where the time goes in v1:
time: 225 us; the launch traced here: 221 us
  waiting for transfers between devices  83.6 us (37%)
  Pallas kernels  48.3 us (21%)
  starting transfers between devices  46.2 us (21%)
  matrix products  16.4 us (7%)
  between operations  14.5 us (6%)
  local copies, waits for them, and re-layouts  10.2 us (5%)
    ppermute x23, waiting for transfers between devices, swap(): lax.ppermute(x, axis, [(i, i ^ distance) for i in range(lax.axis_size(axi...  71.7 us
    ppermute x23, starting transfers between devices, swap(): lax.ppermute(x, axis, [(i, i ^ distance) for i in range(lax.axis_size(axi...  41.7 us
    pallas_call x1, Pallas kernels, local_backward(): pl.pallas_call(local_backward_kernel, grid=(heads,), in_specs=[spec(token...  16.6 us
    all_gather x1, waiting for transfers between devices, body(): w_full = lax.all_gather(w_out, 'head', axis=0, tiled=True)  10.4 us
    pallas_call x1, Pallas kernels, local_forward(): pl.pallas_call(local_forward_kernel, grid=(heads,), in_specs=[spec(tokens...  9.32 us
    dot_general x1, matrix products, body(): mixed = jnp.dot(mine, w_full, preferred_element_type=F32).astype(BF16)  6.7 us
    pallas_call x1, Pallas kernels, coarsen(): pl.pallas_call(coarsen_kernel, grid=(q.shape[1] // HD,), in_specs=[spec(t...  6.26 us
    pallas_call x1, Pallas kernels, coarse_forward(): pl.pallas_call(coarse_forward_kernel, grid=(heads,), in_specs=[lead(token...  5.99 us
  transfers between devices with their start and end apart: 26, of which 13 were waited for; matrix products, arithmetic and copies ran while one was open for 12% of the time, Pallas kernels for 22%

profile of v1, /device:TPU:16, one launch (start us, length us, event | category | flops | bytes accessed | tf_op | source)
XLA Modules:
  0.0 220.9 jit_solution(1309907004950540652)
XLA Ops:
  8.6 6.3 %coarsen.1 = (bf16[2048,256]{1,0:T(8,128)(2,1)}, bf16[2048,256]{1,0:T(8,128)(2,1)}, bf16[2048,256]{1,0:T(8,128)(2,1)}) custom-call(bf16[2048,256]{1,0:T(8,128)(2,1)} %q_ref.5, bf16[2048,256]{1,0:T(8,128)(2,1)} %k_ref.5, bf16[2048,256]{1,0:T(8,128)(2,1)} %v_ref.5), custom_call_target="tpu_custom_call" | custom-call | tf_op jit(solution)/shard_map/coarsen/pallas_call | solution.py:87
  14.9 0.9 slice.222
  15.8 0.9 slice.223
  16.8 3.4 %collective-permute-start.1 = (bf16[120,512]{1,0:T(8,128)(2,1)S(1)}, bf16[120,512]{1,0:T(8,128)(2,1)S(1)}, u32[]{:S(2)}, u32[]{:S(2)}) collective-permute-start(bf16[120,512]{1,0:T(8,128)(2,1)S(1)} %fusion.3), channel_id=1, source_target_pairs={{0,16},{8,24},{16,0},{24,8},{32,48},{40,56},{48,32},{56,40},{64,80... | collective-permute-start | bytes 368648 | tf_op jit(solution)/shard_map/ppermute | solution.py:346
  20.1 1.5 collective-permute-start.2
  22.2 9.3 %local_forward.1 = (f32[2,2048,128]{2,1,0:T(8,128)}, f32[2,2048,128]{2,1,0:T(8,128)}) custom-call(bf16[2048,256]{1,0:T(8,128)(2,1)} %q_ref.5, bf16[2048,256]{1,0:T(8,128)(2,1)} %k_ref.5, bf16[2048,256]{1,0:T(8,128)(2,1)} %v_ref.5, bf16[2048,256]{1,0:T(8,128)(2,1)} %get-tuple-element.22.qc_ref.q_ref, bf16[2048,256]{1,0:T(8,128)(2,1)} %get-tuple-element.23.kc_ref, ...), custom_call_target="tpu_custom_call" | custom-call | tf_op jit(solution)/shard_map/local_forward/pallas_call | solution.py:133
  31.8 1.4 collective-permute-start.4
  33.2 6.6 %collective-permute-start.5 = (bf16[96,512]{1,0:T(8,128)(2,1)S(1)}, bf16[96,512]{1,0:T(8,128)(2,1)S(1)}, u32[]{:S(2)}, u32[]{:S(2)}) collective-permute-start(bf16[96,512]{1,0:T(8,128)(2,1)S(1)} %get-tuple-element.70), channel_id=1, source_target_pairs={{0,96},{8,104},{16,112},{24,120},{32,64},{40,72},{48,80},{56,88},{... | collective-permute-start | bytes 294920 | tf_op jit(solution)/shard_map/ppermute | solution.py:346
  39.9 12.5 %collective-permute-done.3 = bf16[160,512]{1,0:T(8,128)(2,1)S(1)} collective-permute-done((bf16[160,512]{1,0:T(8,128)(2,1)S(1)}, bf16[160,512]{1,0:T(8,128)(2,1)S(1)}, u32[]{:S(2)}, u32[]{:S(2)}) %collective-permute-start.3) | collective-permute-done | bytes 163872 | tf_op jit(solution)/shard_map/ppermute | solution.py:346
  53.1 5.9 %collective-permute-done.6 = bf16[128,512]{1,0:T(8,128)(2,1)S(1)} collective-permute-done((bf16[128,512]{1,0:T(8,128)(2,1)S(1)}, bf16[128,512]{1,0:T(8,128)(2,1)S(1)}, u32[]{:S(2)}, u32[]{:S(2)}) %collective-permute-start.6) | collective-permute-done | bytes 131104 | tf_op jit(solution)/shard_map/ppermute | solution.py:346
  59.0 0.9 fusion.10
  59.9 6.0 %coarse_forward.1 = (bf16[2048,256]{1,0:T(8,128)(2,1)}, f32[2,2048,128]{2,1,0:T(8,128)}) custom-call(f32[2,2048,128]{2,1,0:T(8,128)} %get-tuple-element.25.numer_ref, f32[2,2048,128]{2,1,0:T(8,128)} %get-tuple-element.26.total_ref, bf16[2048,256]{1,0:T(8,128)(2,1)} %get-tuple-element.22.qc_ref.q_ref, bf16[640,256]{1,0:T(8,128)(2,1)} %get-tuple-element.54.k_ref, ...), custom_call_target="tpu_custom_call" | custom-call | tf_op jit(solution)/shard_map/coarse_forward/pallas_call | solution.py:182
  65.9 2.3 %copy.10 = bf16[8,256,256]{1,2,0:T(8,128)(2,1)} copy(bf16[8,256,256]{2,1,0:T(8,128)(2,1)} %bitcast.10) | data formatting | bytes 2097152 | tf_op jit(solution)/shard_map/reshape | solution.py:443
  68.3 4.3 %all-to-all-start = ((bf16[8,256,256]{1,2,0:T(8,128)(2,1)}), bf16[8,256,256]{1,2,0:T(8,128)(2,1)S(1)}, u32[]{:S(2)}, u32[]{:S(2)}) async-start(bf16[8,256,256]{1,2,0:T(8,128)(2,1)} %copy.10), calls=%async_computation | async-start | bytes 2097152 | tf_op jit(solution)/shard_map/all_to_all | solution.py:443
  72.7 5.9 %fusion.17 = f32[256,2048]{1,0:T(8,128)S(1)} fusion(bf16[2048,256]{1,0:T(8,128)(2,1)S(1)} %copy-done.1, bf16[2048,2048]{1,0:T(8,128)(2,1)} %all-gather.5.cloned.1.call-done), kind=kOutput, calls=%fused_computation.91 | convolution fusion | flops 2147483648 | bytes 11534336 | tf_op jit(solution)/shard_map/dot_general | solution.py:28
  78.5 1.0 dynamic-slice_convert_fusion.2
  79.6 1.8 collective-permute-start.14
  82.0 1.1 collective-permute-start.16
  83.1 3.8 %fusion.16.ga_ref = f32[2048,256]{1,0:T(8,128)} fusion(bf16[2048,2048]{1,0:T(8,128)(2,1)S(1)} %copy-done, bf16[256,2048]{1,0:T(8,128)(2,1)S(1)} %copy-done.3), kind=kOutput, calls=%fused_computation.90 | convolution fusion | flops 2147483648 | bytes 11534336 | tf_op jit(solution)/shard_map/dot_general | solution.py:24
  86.9 5.9 %coarse_backward.1 = (bf16[2,2048,256]{2,1,0:T(8,128)(2,1)}, bf16[2,2048,256]{2,1,0:T(8,128)(2,1)}, f32[2,128,128]{2,1,0:T(8,128)}, bf16[640,256]{1,0:T(8,128)(2,1)}, bf16[640,256]{1,0:T(8,128)(2,1)}) custom-call(f32[2048,256]{1,0:T(8,128)} %fusion.16.ga_ref, bf16[2048,256]{1,0:T(8,128)(2,1)} %get-tuple-element.27.att_ref, ...), custom_call_target="tpu_custom_call" | custom-call | tf_op jit(solution)/shard_map/coarse_backward/pallas_call | solution.py:260
  92.8 1.0 constant_dynamic-update-slice_fusion.29
  93.8 1.0 constant_dynamic-update-slice_fusion.28
  94.8 1.9 collective-permute-start.7
  96.8 16.6 %local_backward.1 = (bf16[2048,256]{1,0:T(8,128)(2,1)}, bf16[2048,256]{1,0:T(8,128)(2,1)}, bf16[2048,256]{1,0:T(8,128)(2,1)}) custom-call(bf16[2048,256]{1,0:T(8,128)(2,1)} %q_ref.5, bf16[2048,256]{1,0:T(8,128)(2,1)} %k_ref.5, bf16[2048,256]{1,0:T(8,128)(2,1)} %v_ref.5, bf16[2048,256]{1,0:T(8,128)(2,1)} %get-tuple-element.22.qc_ref.q_ref, ...), custom_call_target="tpu_custom_call" | custom-call | tf_op jit(solution)/shard_map/local_backward/pallas_call | solution.py:312
  113.4 10.4 %all-gather.3.cloned.1.call-done = bf16[2048,2048]{1,0:T(8,128)(2,1)} async-done(((bf16[256,2048]{1,0:T(8,128)(2,1)}), bf16[2048,2048]{1,0:T(8,128)(2,1)}) %all-gather.3.cloned.1.call-update) | async-done | bytes 8388624 | tf_op jit(solution)/shard_map/all_gather | solution.py:435
  123.8 6.7 %convolution_convert_fusion = bf16[256,2048]{1,0:T(8,128)(2,1)} fusion(bf16[256,2048]{0,1:T(8,128)(2,1)S(1)} %bitcast.11, bf16[2048,2048]{1,0:T(8,128)(2,1)} %all-gather.3.cloned.1.call-done), kind=kOutput, calls=%fused_computation | convolution fusion | flops 2148007936 | bytes 10485760 | tf_op jit(solution)/shard_map/dot_general | solution.py:445
  130.6 1.9 collective-permute-start.9
  132.5 4.2 %collective-permute-start.10 = (bf16[96,512]{1,0:T(8,128)(2,1)S(1)}, bf16[96,512]{1,0:T(8,128)(2,1)S(1)}, u32[]{:S(2)}, u32[]{:S(2)}) collective-permute-start(bf16[96,512]{1,0:T(8,128)(2,1)S(1)} %pad_maximum_fusion.6), channel_id=1, source_target_pairs={{0,96},{8,104},{16,112},{24,120},{32,64},{40,72},{48,80},{56,88},{... | collective-permute-start | bytes 294920 | tf_op jit(solution)/shard_map/ppermute | solution.py:346
  136.7 3.4 %collective-permute-start.8 = (bf16[160,512]{1,0:T(8,128)(2,1)S(1)}, bf16[160,512]{1,0:T(8,128)(2,1)S(1)}, u32[]{:S(2)}, u32[]{:S(2)}) collective-permute-start(bf16[160,512]{1,0:T(8,128)(2,1)S(1)} %pad_maximum_fusion.2), channel_id=1, source_target_pairs={{0,32},{8,40},{16,48},{24,56},{32,0},{40,8},{48,16},{56,24},{64,96... | collective-permute-start | bytes 491528 | tf_op jit(solution)/shard_map/ppermute | solution.py:346
  140.1 5.5 %collective-permute-done.10 = bf16[96,512]{1,0:T(8,128)(2,1)S(1)} collective-permute-done((bf16[96,512]{1,0:T(8,128)(2,1)S(1)}, bf16[96,512]{1,0:T(8,128)(2,1)S(1)}, u32[]{:S(2)}, u32[]{:S(2)}) %collective-permute-start.10) | collective-permute-done | bytes 98336 | tf_op jit(solution)/shard_map/ppermute | solution.py:346
  145.6 1.3 fusion.7
  147.1 2.0 collective-permute-done.8
  149.2 1.9 collective-permute-start.11
  151.4 2.4 %collective-permute-start.13 = (bf16[120,512]{1,0:T(8,128)(2,1)S(1)}, bf16[120,512]{1,0:T(8,128)(2,1)S(1)}, u32[]{:S(2)}, u32[]{:S(2)}) collective-permute-start(bf16[120,512]{1,0:T(8,128)(2,1)S(1)} %pad_maximum_fusion.4), channel_id=1, source_target_pairs={{0,24},{8,16},{16,8},{24,0},{32,56},{40,48},{48,40},{56,32},{64,88... | collective-permute-start | bytes 368648 | tf_op jit(solution)/shard_map/ppermute | solution.py:346
  153.8 7.7 %collective-permute-done.11 = bf16[184,512]{1,0:T(8,128)(2,1)S(1)} collective-permute-done((bf16[184,512]{1,0:T(8,128)(2,1)S(1)}, bf16[184,512]{1,0:T(8,128)(2,1)S(1)}, u32[]{:S(2)}, u32[]{:S(2)}) %collective-permute-start.11) | collective-permute-done | bytes 188448 | tf_op jit(solution)/shard_map/ppermute | solution.py:346
  161.8 2.8 %collective-permute-done.13 = bf16[120,512]{1,0:T(8,128)(2,1)S(1)} collective-permute-done((bf16[120,512]{1,0:T(8,128)(2,1)S(1)}, bf16[120,512]{1,0:T(8,128)(2,1)S(1)}, u32[]{:S(2)}, u32[]{:S(2)}) %collective-permute-start.13) | collective-permute-done | bytes 122912 | tf_op jit(solution)/shard_map/ppermute | solution.py:346
  164.7 10.7 %collective-permute-done.18 = bf16[64,2048]{1,0:T(8,128)(2,1)S(1)} collective-permute-done((bf16[64,2048]{1,0:T(8,128)(2,1)S(1)}, bf16[64,2048]{1,0:T(8,128)(2,1)S(1)}, u32[]{:S(2)}, u32[]{:S(2)}) %collective-permute-start.18) | collective-permute-done | bytes 262176 | tf_op jit(solution)/shard_map/ppermute | solution.py:346
  175.5 4.5 %collective-permute-start.19 = (bf16[64,2048]{1,0:T(8,128)(2,1)S(1)}, bf16[64,2048]{1,0:T(8,128)(2,1)S(1)}, u32[]{:S(2)}, u32[]{:S(2)}) collective-permute-start(bf16[64,2048]{1,0:T(8,128)(2,1)S(1)} %fusion.1), channel_id=1, source_target_pairs={{0,32},{8,40},{16,48},{24,56},{32,0},{40,8},{48,16},{56,24},{64,96... | collective-permute-start | bytes 786440 | tf_op jit(solution)/shard_map/ppermute | solution.py:346
  180.0 13.3 %collective-permute-done.19 = bf16[64,2048]{1,0:T(8,128)(2,1)S(1)} collective-permute-done((bf16[64,2048]{1,0:T(8,128)(2,1)S(1)}, bf16[64,2048]{1,0:T(8,128)(2,1)S(1)}, u32[]{:S(2)}, u32[]{:S(2)}) %collective-permute-start.19) | collective-permute-done | bytes 262176 | tf_op jit(solution)/shard_map/ppermute | solution.py:346
  193.6 1.4 collective-permute-start.20
  194.9 0.9 collective-permute-start.21
  195.8 0.7 fusion.11
  196.5 4.2 %finish.1 = (bf16[2048,256]{1,0:T(8,128)(2,1)}, bf16[2048,256]{1,0:T(8,128)(2,1)}) custom-call(bf16[2048,256]{1,0:T(8,128)(2,1)} %get-tuple-element.33.dk_ref, bf16[2048,256]{1,0:T(8,128)(2,1)} %get-tuple-element.34.dv_ref, bf16[256,256]{1,0:T(8,128)(2,1)} %get-tuple-element.56.ck_ref, bf16[256,256]{1,0:T(8,128)(2,1)} %get-tuple-element.55.cv_ref), custom_call_target="tpu_custom_call" | custom-call | tf_op jit(solution)/shard_map/finish/pallas_call | solution.py:333
  200.8 1.4 collective-permute-start.22
  202.1 0.8 collective-permute-done.20
  202.9 4.7 %collective-permute-done.21 = bf16[64,2048]{1,0:T(8,128)(2,1)S(1)} collective-permute-done((bf16[64,2048]{1,0:T(8,128)(2,1)S(1)}, bf16[64,2048]{1,0:T(8,128)(2,1)S(1)}, u32[]{:S(2)}, u32[]{:S(2)}) %collective-permute-start.21) | collective-permute-done | bytes 262176 | tf_op jit(solution)/shard_map/ppermute | solution.py:346
  207.7 5.4 %collective-permute-done.22 = bf16[64,2048]{1,0:T(8,128)(2,1)S(1)} collective-permute-done((bf16[64,2048]{1,0:T(8,128)(2,1)S(1)}, bf16[64,2048]{1,0:T(8,128)(2,1)S(1)}, u32[]{:S(2)}, u32[]{:S(2)}) %collective-permute-start.22) | collective-permute-done | bytes 262176 | tf_op jit(solution)/shard_map/ppermute | solution.py:346
  213.1 1.0 copy-done.4
  (87 shorter events, 4.8 us)
Async XLA Ops:
  7.2 65.5 %all-gather.5.cloned.1.call-start = ((), (), s32[]{:S(2)}) async-start(), calls=%async_computation.2 | async-start | bytes 9437184 | tf_op jit(solution)/shard_map/all_gather | solution.py:434
  7.9 115.9 %all-gather.3.cloned.1.call-start = ((), (), s32[]{:S(2)}) async-start(), calls=%async_computation.1 | async-start | bytes 9437184 | tf_op jit(solution)/shard_map/all_gather | solution.py:435
  16.8 14.9 %collective-permute-start.1 = (bf16[120,512]{1,0:T(8,128)(2,1)S(1)}, bf16[120,512]{1,0:T(8,128)(2,1)S(1)}, u32[]{:S(2)}, u32[]{:S(2)}) collective-permute-start(bf16[120,512]{1,0:T(8,128)(2,1)S(1)} %fusion.3), channel_id=1, source_target_pairs={{0,16},{8,24},{16,0},{24,8},{32,48},{40,56},{48,32},{56,40},{64,80... | collective-permute-start | bytes 368648 | tf_op jit(solution)/shard_map/ppermute | solution.py:346
  20.1 11.6 %collective-permute-start.2 = (bf16[120,512]{1,0:T(8,128)(2,1)S(1)}, bf16[120,512]{1,0:T(8,128)(2,1)S(1)}, u32[]{:S(2)}, u32[]{:S(2)}) collective-permute-start(bf16[120,512]{1,0:T(8,128)(2,1)S(1)} %fusion.3), channel_id=1, source_target_pairs={{0,24},{8,16},{16,8},{24,0},{32,56},{40,48},{48,40},{56,32},{64,88... | collective-permute-start | bytes 368648 | tf_op jit(solution)/shard_map/ppermute | solution.py:346
  21.6 10.1 %collective-permute-start = (bf16[184,512]{1,0:T(8,128)(2,1)S(1)}, bf16[184,512]{1,0:T(8,128)(2,1)S(1)}, u32[]{:S(2)}, u32[]{:S(2)}) collective-permute-start(bf16[184,512]{1,0:T(8,128)(2,1)S(1)} %pad_maximum_fusion), channel_id=1, source_target_pairs={{0,8},{8,0},{16,24},{24,16},{32,40},{40,32},{48,56},{56,48},{64,72... | collective-permute-start | bytes 565256 | tf_op jit(solution)/shard_map/ppermute | solution.py:346
  31.8 20.6 %collective-permute-start.4 = (bf16[96,512]{1,0:T(8,128)(2,1)S(1)}, bf16[96,512]{1,0:T(8,128)(2,1)S(1)}, u32[]{:S(2)}, u32[]{:S(2)}) collective-permute-start(bf16[96,512]{1,0:T(8,128)(2,1)S(1)} %get-tuple-element.70), channel_id=1, source_target_pairs={{0,64},{8,72},{16,80},{24,88},{32,96},{40,104},{48,112},{56,120},{... | collective-permute-start | bytes 294920 | tf_op jit(solution)/shard_map/ppermute | solution.py:346
  33.2 19.2 %collective-permute-start.5 = (bf16[96,512]{1,0:T(8,128)(2,1)S(1)}, bf16[96,512]{1,0:T(8,128)(2,1)S(1)}, u32[]{:S(2)}, u32[]{:S(2)}) collective-permute-start(bf16[96,512]{1,0:T(8,128)(2,1)S(1)} %get-tuple-element.70), channel_id=1, source_target_pairs={{0,96},{8,104},{16,112},{24,120},{32,64},{40,72},{48,80},{56,88},{... | collective-permute-start | bytes 294920 | tf_op jit(solution)/shard_map/ppermute | solution.py:346
  39.8 12.6 %collective-permute-start.3 = (bf16[160,512]{1,0:T(8,128)(2,1)S(1)}, bf16[160,512]{1,0:T(8,128)(2,1)S(1)}, u32[]{:S(2)}, u32[]{:S(2)}) collective-permute-start(bf16[160,512]{1,0:T(8,128)(2,1)S(1)} %get-tuple-element.71), channel_id=1, source_target_pairs={{0,32},{8,40},{16,48},{24,56},{32,0},{40,8},{48,16},{56,24},{64,96... | collective-permute-start | bytes 491528 | tf_op jit(solution)/shard_map/ppermute | solution.py:346
  52.5 6.6 %collective-permute-start.6 = (bf16[128,512]{1,0:T(8,128)(2,1)S(1)}, bf16[128,512]{1,0:T(8,128)(2,1)S(1)}, u32[]{:S(2)}, u32[]{:S(2)}) collective-permute-start(bf16[128,512]{1,0:T(8,128)(2,1)S(1)} %constant_dynamic-update-slice_fusion.16), channel_id=1, source_target_pairs={{0,128},{8,136},{16,144},{24,152},{32,160},{40,168},{48,176},{56,1... | collective-permute-start | bytes 393224 | tf_op jit(solution)/shard_map/ppermute | solution.py:346
  65.9 6.7 %copy-start.1 = (bf16[2048,256]{1,0:T(8,128)(2,1)S(1)}, bf16[2048,256]{1,0:T(8,128)(2,1)}, u32[]{:S(2)}) copy-start(bf16[2048,256]{1,0:T(8,128)(2,1)} %get-tuple-element.27.att_ref) | copy-start | bytes 3145732
  68.3 45.1 %all-to-all-start = ((bf16[8,256,256]{1,2,0:T(8,128)(2,1)}), bf16[8,256,256]{1,2,0:T(8,128)(2,1)S(1)}, u32[]{:S(2)}, u32[]{:S(2)}) async-start(bf16[8,256,256]{1,2,0:T(8,128)(2,1)} %copy.10), calls=%async_computation | async-start | bytes 2097152 | tf_op jit(solution)/shard_map/all_to_all | solution.py:443
  72.6 10.5 %copy-start.3 = (bf16[256,2048]{1,0:T(8,128)(2,1)S(1)}, bf16[256,2048]{1,0:T(8,128)(2,1)}, u32[]{:S(2)}) copy-start(bf16[256,2048]{1,0:T(8,128)(2,1)} %param.8) | copy-start | bytes 3145732
  72.7 10.4 %copy-start = (bf16[2048,2048]{1,0:T(8,128)(2,1)S(1)}, bf16[2048,2048]{1,0:T(8,128)(2,1)}, u32[]{:S(2)}) copy-start(bf16[2048,2048]{1,0:T(8,128)(2,1)} %all-gather.5.cloned.1.call-done) | copy-start | bytes 25165828
  78.5 8.4 %copy-start.2 = (f32[256,2048]{1,0:T(8,128)}, f32[256,2048]{1,0:T(8,128)S(1)}, u32[]{:S(2)}) copy-start(f32[256,2048]{1,0:T(8,128)S(1)} %fusion.17) | copy-start | bytes 6291460
  79.6 66.0 %collective-permute-start.14 = (bf16[64,2048]{1,0:T(8,128)(2,1)}, bf16[64,2048]{1,0:T(8,128)(2,1)S(1)}, u32[]{:S(2)}, u32[]{:S(2)}) collective-permute-start(bf16[64,2048]{1,0:T(8,128)(2,1)} %get-tuple-element.43), channel_id=1, source_target_pairs={{0,64},{8,72},{16,80},{24,88},{32,96},{40,104},{48,112},{56,120},{... | collective-permute-start | bytes 786440 | tf_op jit(solution)/shard_map/ppermute | solution.py:346
  81.4 64.2 %collective-permute-start.15 = (bf16[64,2048]{1,0:T(8,128)(2,1)}, bf16[64,2048]{1,0:T(8,128)(2,1)}, u32[]{:S(2)}, u32[]{:S(2)}) collective-permute-start(bf16[64,2048]{1,0:T(8,128)(2,1)} %get-tuple-element.45), channel_id=1, source_target_pairs={{0,128},{8,136},{16,144},{24,152},{32,160},{40,168},{48,176},{56,1... | collective-permute-start | bytes 786440 | tf_op jit(solution)/shard_map/ppermute | solution.py:346
  82.0 63.6 %collective-permute-start.16 = (bf16[64,2048]{1,0:T(8,128)(2,1)}, bf16[64,2048]{1,0:T(8,128)(2,1)}, u32[]{:S(2)}, u32[]{:S(2)}) collective-permute-start(bf16[64,2048]{1,0:T(8,128)(2,1)} %get-tuple-element.44), channel_id=1, source_target_pairs={{0,192},{8,200},{16,208},{24,216},{32,224},{40,232},{48,240},{56,2... | collective-permute-start | bytes 786440 | tf_op jit(solution)/shard_map/ppermute | solution.py:346
  94.8 35.7 %collective-permute-start.7 = (bf16[128,512]{1,0:T(8,128)(2,1)S(1)}, bf16[128,512]{1,0:T(8,128)(2,1)S(1)}, u32[]{:S(2)}, u32[]{:S(2)}) collective-permute-start(bf16[128,512]{1,0:T(8,128)(2,1)S(1)} %get-tuple-element.51), channel_id=1, source_target_pairs={{0,128},{8,136},{16,144},{24,152},{32,160},{40,168},{48,176},{56,1... | collective-permute-start | bytes 393224 | tf_op jit(solution)/shard_map/ppermute | solution.py:346
  130.6 6.1 %collective-permute-start.9 = (bf16[96,512]{1,0:T(8,128)(2,1)S(1)}, bf16[96,512]{1,0:T(8,128)(2,1)S(1)}, u32[]{:S(2)}, u32[]{:S(2)}) collective-permute-start(bf16[96,512]{1,0:T(8,128)(2,1)S(1)} %pad_maximum_fusion.5), channel_id=1, source_target_pairs={{0,64},{8,72},{16,80},{24,88},{32,96},{40,104},{48,112},{56,120},{... | collective-permute-start | bytes 294920 | tf_op jit(solution)/shard_map/ppermute | solution.py:346
  132.5 13.1 %collective-permute-start.10 = (bf16[96,512]{1,0:T(8,128)(2,1)S(1)}, bf16[96,512]{1,0:T(8,128)(2,1)S(1)}, u32[]{:S(2)}, u32[]{:S(2)}) collective-permute-start(bf16[96,512]{1,0:T(8,128)(2,1)S(1)} %pad_maximum_fusion.6), channel_id=1, source_target_pairs={{0,96},{8,104},{16,112},{24,120},{32,64},{40,72},{48,80},{56,88},{... | collective-permute-start | bytes 294920 | tf_op jit(solution)/shard_map/ppermute | solution.py:346
  136.7 12.4 %collective-permute-start.8 = (bf16[160,512]{1,0:T(8,128)(2,1)S(1)}, bf16[160,512]{1,0:T(8,128)(2,1)S(1)}, u32[]{:S(2)}, u32[]{:S(2)}) collective-permute-start(bf16[160,512]{1,0:T(8,128)(2,1)S(1)} %pad_maximum_fusion.2), channel_id=1, source_target_pairs={{0,32},{8,40},{16,48},{24,56},{32,0},{40,8},{48,16},{56,24},{64,96... | collective-permute-start | bytes 491528 | tf_op jit(solution)/shard_map/ppermute | solution.py:346
  147.0 14.6 %collective-permute-start.17 = (bf16[64,2048]{1,0:T(8,128)(2,1)S(1)}, bf16[64,2048]{1,0:T(8,128)(2,1)S(1)}, u32[]{:S(2)}, u32[]{:S(2)}) collective-permute-start(bf16[64,2048]{1,0:T(8,128)(2,1)S(1)} %get-tuple-element.41), channel_id=1, source_target_pairs={{0,8},{8,0},{16,24},{24,16},{32,40},{40,32},{48,56},{56,48},{64,72... | collective-permute-start | bytes 786440 | tf_op jit(solution)/shard_map/ppermute | solution.py:346
  149.2 12.4 %collective-permute-start.11 = (bf16[184,512]{1,0:T(8,128)(2,1)S(1)}, bf16[184,512]{1,0:T(8,128)(2,1)S(1)}, u32[]{:S(2)}, u32[]{:S(2)}) collective-permute-start(bf16[184,512]{1,0:T(8,128)(2,1)S(1)} %pad_maximum_fusion.1), channel_id=1, source_target_pairs={{0,8},{8,0},{16,24},{24,16},{32,40},{40,32},{48,56},{56,48},{64,72... | collective-permute-start | bytes 565256 | tf_op jit(solution)/shard_map/ppermute | solution.py:346
  151.1 10.7 %collective-permute-start.12 = (bf16[120,512]{1,0:T(8,128)(2,1)S(1)}, bf16[120,512]{1,0:T(8,128)(2,1)S(1)}, u32[]{:S(2)}, u32[]{:S(2)}) collective-permute-start(bf16[120,512]{1,0:T(8,128)(2,1)S(1)} %pad_maximum_fusion.3), channel_id=1, source_target_pairs={{0,16},{8,24},{16,0},{24,8},{32,48},{40,56},{48,32},{56,40},{64,80... | collective-permute-start | bytes 368648 | tf_op jit(solution)/shard_map/ppermute | solution.py:346
  151.4 13.2 %collective-permute-start.13 = (bf16[120,512]{1,0:T(8,128)(2,1)S(1)}, bf16[120,512]{1,0:T(8,128)(2,1)S(1)}, u32[]{:S(2)}, u32[]{:S(2)}) collective-permute-start(bf16[120,512]{1,0:T(8,128)(2,1)S(1)} %pad_maximum_fusion.4), channel_id=1, source_target_pairs={{0,24},{8,16},{16,8},{24,0},{32,56},{40,48},{48,40},{56,32},{64,88... | collective-permute-start | bytes 368648 | tf_op jit(solution)/shard_map/ppermute | solution.py:346
  161.7 13.7 %collective-permute-start.18 = (bf16[64,2048]{1,0:T(8,128)(2,1)S(1)}, bf16[64,2048]{1,0:T(8,128)(2,1)S(1)}, u32[]{:S(2)}, u32[]{:S(2)}) collective-permute-start(bf16[64,2048]{1,0:T(8,128)(2,1)S(1)} %fusion), channel_id=1, source_target_pairs={{0,16},{8,24},{16,0},{24,8},{32,48},{40,56},{48,32},{56,40},{64,80... | collective-permute-start | bytes 786440 | tf_op jit(solution)/shard_map/ppermute | solution.py:346
  175.5 17.8 %collective-permute-start.19 = (bf16[64,2048]{1,0:T(8,128)(2,1)S(1)}, bf16[64,2048]{1,0:T(8,128)(2,1)S(1)}, u32[]{:S(2)}, u32[]{:S(2)}) collective-permute-start(bf16[64,2048]{1,0:T(8,128)(2,1)S(1)} %fusion.1), channel_id=1, source_target_pairs={{0,32},{8,40},{16,48},{24,56},{32,0},{40,8},{48,16},{56,24},{64,96... | collective-permute-start | bytes 786440 | tf_op jit(solution)/shard_map/ppermute | solution.py:346
  193.6 9.3 %collective-permute-start.20 = (bf16[64,2048]{1,0:T(8,128)(2,1)S(1)}, bf16[64,2048]{1,0:T(8,128)(2,1)S(1)}, u32[]{:S(2)}, u32[]{:S(2)}) collective-permute-start(bf16[64,2048]{1,0:T(8,128)(2,1)S(1)} %get-tuple-element.40), channel_id=1, source_target_pairs={{0,64},{8,72},{16,80},{24,88},{32,96},{40,104},{48,112},{56,120},{... | collective-permute-start | bytes 786440 | tf_op jit(solution)/shard_map/ppermute | solution.py:346
  194.9 12.7 %collective-permute-start.21 = (bf16[64,2048]{1,0:T(8,128)(2,1)S(1)}, bf16[64,2048]{1,0:T(8,128)(2,1)S(1)}, u32[]{:S(2)}, u32[]{:S(2)}) collective-permute-start(bf16[64,2048]{1,0:T(8,128)(2,1)S(1)} %get-tuple-element.40), channel_id=1, source_target_pairs={{0,128},{8,136},{16,144},{24,152},{32,160},{40,168},{48,176},{56,1... | collective-permute-start | bytes 786440 | tf_op jit(solution)/shard_map/ppermute | solution.py:346
  200.8 12.3 %collective-permute-start.22 = (bf16[64,2048]{1,0:T(8,128)(2,1)S(1)}, bf16[64,2048]{1,0:T(8,128)(2,1)S(1)}, u32[]{:S(2)}, u32[]{:S(2)}) collective-permute-start(bf16[64,2048]{1,0:T(8,128)(2,1)S(1)} %get-tuple-element.40), channel_id=1, source_target_pairs={{0,192},{8,200},{16,208},{24,216},{32,224},{40,232},{48,240},{56,2... | collective-permute-start | bytes 786440 | tf_op jit(solution)/shard_map/ppermute | solution.py:346
  213.1 1.0 copy-start.4
Sparse Core Ops, SparseCore 0:
  9.9 55.0 all-gather.4
  66.8 56.9 all-gather.2
